TPU v7x, 32 devices: a whole 2x2x4 slice. The times are simulated.
32 devices in a mesh: groups: 2 (over y), pack: 4 (over z), mp: 2 (over x), sub: 2 (over core).
Axes of the slice: x: 2, y: 2, z: 4, core: 2. Of those that a mesh axis runs over, the one named last changes fastest.
Arguments:
- frame_enc: bfloat16 [8192, 512], P(('groups', 'pack')), parts along dimension 0, may hold values from -400 to 400
- phrase_enc: bfloat16 [16384, 1024], P(('groups', 'pack', 'mp')), parts along dimension 0, may hold values from -6 to 6
- key_weight: bfloat16 [1024, 512], replicated, may hold values from -0.1875 to 0.1875
- out_weight: bfloat16 [512, 4096], P(None, ('mp', 'sub')), may hold values from -1.5 to 1.5
- gate_weight: float32 [512], replicated, may hold values from -0.5 to 0.5
- phrase_token: int32 [16384], P('groups'), parts along dimension 0, may hold values from 1 to 4095
- bias_blocks: int32 [8, 128], P('groups'), parts along dimension 0, may hold values from 0 to 127, as said below
- utt_lengths: int32 [8, 4], P(('groups', 'pack')), parts along dimension 0, may hold values from 1 to 512, 1024 in all within a row
- targets: int32 [8192], P(('groups', 'pack')), parts along dimension 0, may hold values from 0 to 4095
Outputs:
- loss: float32 [8192], P(('groups', 'pack')), parts along dimension 0
There are 2 independent parts, one for each index of `groups`. A program takes and returns all parts, laid end to end along the dimension named above; an argument that names none is the same for every part. Nothing has to cross between parts.
Inputs may be any that keep to these rules, and one draw needn't show every extreme that they name: `bias_blocks`: in every row, at most 32 entries lie in one phrase shard (equal values of block // 16), and some shard gives exactly 32 entries to every row. `utt_lengths`: each row sums to 1024.
All inputs are finite; a program needn't handle non-finite values.
Results may differ from a plain program's by a relative error of at most 0.0016.
Values may be sent and summed in bfloat16 or wider, within the bound.
A program may use at most 128 MiB of HBM per device.

v0:
```python
import math

import jax
import jax.numpy as jnp
from jax import lax
from jax.sharding import PartitionSpec as P

BLK = 64


score_gain = 2.0
masked_low = -1e30


def joined(shard, axis, combine):
    everything = jax.tree.map(lambda part: lax.all_gather(part, axis), shard)
    initial = jax.tree.map(lambda part: part[0], everything)

    def step(k, so_far):
        return combine(so_far, jax.tree.map(lambda part: part[k], everything))

    return lax.fori_loop(1, lax.axis_size(axis), step, initial)


def vocab_join(first, second):
    joined_top = jnp.maximum(first[0], second[0])
    joined_sum = first[1] * jnp.exp(first[0] - joined_top) + second[1] * jnp.exp(
        second[0] - joined_top
    )
    return (joined_top, joined_sum, first[2] + second[2])


def per_device(
    frame_enc,
    phrase_enc,
    key_weight,
    out_weight,
    gate_weight,
    phrase_token,
    bias_blocks,
    utt_lengths,
    targets,
):
    pack_count = lax.axis_size("pack")
    mp_count = lax.axis_size("mp")
    sub_count = lax.axis_size("sub")
    pack_index = lax.axis_index("pack")
    mp_index = lax.axis_index("mp")
    frames, width = frame_enc.shape
    packs, entries = bias_blocks.shape
    utt_count = utt_lengths.shape[1]
    list_blocks = entries // utt_count
    shard_blocks = phrase_enc.shape[0] // BLK
    capacity = 2 * entries // (pack_count * mp_count)
    device = pack_index * mp_count + mp_index
    phrase_keys = jnp.dot(phrase_enc, key_weight, preferred_element_type=jnp.float32).astype(
        jnp.bfloat16
    )
    key_blocks = phrase_keys.reshape(shard_blocks, BLK * width)
    source = bias_blocks // shard_blocks
    positions = jnp.arange(entries, dtype=jnp.int32)
    earlier = positions[None, :] < positions[:, None]
    source_rank = jnp.sum(
        (source[:, :, None] == source[:, None, :]) & earlier[None], axis=2, dtype=jnp.int32
    )
    slot_ids = jnp.arange(capacity, dtype=jnp.int32)
    selected = (
        (source == device)[:, :, None, None]
        & (source_rank[:, :, None, None] == slot_ids[None, None, :, None])
        & (
            (bias_blocks % shard_blocks)[:, :, None, None]
            == jnp.arange(shard_blocks, dtype=jnp.int32)[None, None, None, :]
        )
    )
    chooser = jnp.any(selected, axis=1).astype(jnp.bfloat16).reshape(packs * capacity, shard_blocks)
    outgoing = jnp.dot(chooser, key_blocks, preferred_element_type=jnp.float32).astype(jnp.bfloat16)
    outgoing = outgoing.reshape(packs, capacity, BLK, width)
    arrived = lax.all_to_all(outgoing, "pack", split_axis=0, concat_axis=0, tiled=True)
    slot_keys = arrived.reshape(packs * capacity * BLK, width)
    own_blocks = lax.dynamic_index_in_dim(bias_blocks, pack_index, 0, keepdims=False)
    own_source = lax.dynamic_index_in_dim(source, pack_index, 0, keepdims=False)
    own_rank = lax.dynamic_index_in_dim(source_rank, pack_index, 0, keepdims=False)
    sender = jnp.arange(pack_count, dtype=jnp.int32) * mp_count + mp_index
    matched = (own_source[None, None, :] == sender[:, None, None]) & (
        own_rank[None, None, :] == slot_ids[None, :, None]
    )
    filled = jnp.any(matched, axis=2)
    owner_utt = positions // list_blocks
    slot_utt = jnp.where(
        filled,
        jnp.sum(jnp.where(matched, owner_utt[None, None, :], 0), axis=2, dtype=jnp.int32),
        -1,
    )
    slot_block = jnp.sum(jnp.where(matched, own_blocks[None, None, :], 0), axis=2, dtype=jnp.int32)
    slot_token = jnp.take(
        phrase_token,
        (slot_block[:, :, None] * BLK + jnp.arange(BLK, dtype=jnp.int32)[None, None, :]).reshape(
            -1
        ),
    )
    slot_utt = jnp.broadcast_to(slot_utt[:, :, None], (packs, capacity, BLK)).reshape(-1)
    utt_ends = jnp.cumsum(utt_lengths[0], dtype=jnp.int32)
    frame_utt = jnp.sum(
        jnp.arange(frames, dtype=jnp.int32)[:, None] >= utt_ends[None, :], axis=1, dtype=jnp.int32
    )
    scale = score_gain / math.sqrt(width)
    scores = (
        lax.dot_general(
            frame_enc, slot_keys, (((1,), (1,)), ((), ())), preferred_element_type=jnp.float32
        )
        * scale
    )
    visible = frame_utt[:, None] == slot_utt[None, :]
    target_hit = visible & (slot_token[None, :] == targets[:, None])
    masked = jnp.where(visible, scores, masked_low)
    local_top = jnp.max(masked, axis=1)
    row_top = lax.pmax(local_top, "mp")
    row_exp = jnp.where(visible, jnp.exp(masked - row_top[:, None]), 0.0)
    row_total, pointer = lax.psum(
        (jnp.sum(row_exp, axis=1), jnp.sum(jnp.where(target_hit, row_exp, 0.0), axis=1)), "mp"
    )
    weights = (row_exp / row_total[:, None]).astype(jnp.bfloat16)
    partial_value = jnp.dot(weights, slot_keys, preferred_element_type=jnp.float32)
    context = lax.psum(partial_value, "mp")
    hidden = jnp.tanh(frame_enc.astype(jnp.float32) + context).astype(jnp.bfloat16)
    gate_prob = jax.nn.sigmoid(jnp.sum(hidden.astype(jnp.float32) * gate_weight[None, :], axis=1))
    logits = jnp.dot(hidden, out_weight, preferred_element_type=jnp.float32)
    vocab_cols = logits.shape[1]
    first_col = (mp_index * sub_count + lax.axis_index("sub")) * vocab_cols
    local_max = jnp.max(logits, axis=1)
    local_sum = jnp.sum(jnp.exp(logits - local_max[:, None]), axis=1)
    column_ids = jnp.arange(vocab_cols, dtype=jnp.int32)[None, :] + first_col
    chosen = jnp.sum(jnp.where(column_ids == targets[:, None], logits, 0.0), axis=1)
    vocab_top, vocab_total, target_logit = joined(
        (local_max, local_sum, chosen), ("mp", "sub"), vocab_join
    )
    log_norm = vocab_top + jnp.log(vocab_total)
    mixed = (1.0 - gate_prob) * jnp.exp(target_logit - log_norm) + gate_prob * (pointer / row_total)
    return -jnp.log(mixed)


def solution(mesh):
    in_specs = (
        P(("groups", "pack"), None),
        P(("groups", "pack", "mp"), None),
        P(),
        P(None, ("mp", "sub")),
        P(),
        P("groups"),
        P("groups", None),
        P(("groups", "pack"), None),
        P(("groups", "pack")),
    )
    out_specs = P(("groups", "pack"))
    return jax.shard_map(
        per_device, mesh=mesh, in_specs=in_specs, out_specs=out_specs, check_vma=False
    )
```

profile of v0, /device:TPU:0, one launch (start us, length us, event | category | flops | bytes accessed | tf_op | source)
XLA Modules:
  0.0 382.1 jit_solution(3871919648811288619)
XLA Ops:
  6.5 0.0 copy-start
  6.6 0.8 add_select_fusion
  7.4 0.7 broadcast_compare_fusion
  8.1 0.0 copy-done
  8.1 2.5 convolution_convert_fusion.1
  10.6 0.5 reshape.232
  11.1 0.2 convert_reduce_fusion
  11.4 2.3 and_reduce_fusion
  13.7 5.5 %convolution_convert_fusion = bf16[128,32768]{1,0:T(8,128)(2,1)} fusion(pred[128,16]{1,0:T(8,128)(4,1)S(1)} %bitcast.50, bf16[16,32768]{1,0:T(8,128)(2,1)S(1)} %reshape.232), kind=kOutput, calls=%fused_computation.8 | convolution fusion | flops 138412032 | bytes 9439232 | tf_op jit(solution)/shard_map/dot_general | solution.py:76
  19.2 10.1 %copy.10 = bf16[16,8,64,512]{3,2,1,0:T(8,128)(2,1)} copy(bf16[16,8,64,512]{3,1,2,0:T(8,128)(2,1)} %bitcast.45) | data formatting | bytes 16777216
  29.3 0.0 copy-start.6
  29.3 0.0 copy-start.2
  29.3 6.5 %all-to-all-start = ((bf16[4,32,64,512]{3,2,1,0:T(8,128)(2,1)}), bf16[4,32,64,512]{3,2,1,0:T(8,128)(2,1)}, u32[]{:S(2)}, u32[]{:S(2)}) async-start(bf16[4,32,64,512]{3,2,1,0:T(8,128)(2,1)} %bitcast.44), calls=%async_computation | async-start | bytes 16777216 | tf_op jit(solution)/shard_map/all_to_all | solution.py:78
  35.8 0.0 all-reduce.3.cloned.1.call-start
  35.8 0.7 fusion.8
  36.5 0.1 broadcast_compare_fusion.1
  36.6 0.2 fusion.2
  36.8 0.1 iota_add_fusion
  36.9 0.1 add.193
  37.0 0.1 add.190
  37.1 0.2 and_reduce_fusion.1
  37.3 0.1 broadcast_in_dim.46
  37.3 0.1 eq.147
  37.4 0.0 copy-done.6
  37.4 0.2 reduce-window.8
  37.7 0.0 copy-done.2
  37.7 0.0 copy-start.3
  37.7 45.5 %gather_fusion = s32[8192]{0:T(1024)S(1)} fusion(s32[8192]{0:T(1024)S(1)} %copy-done.2, s32[8192]{0:T(1024)S(1)} %broadcast_clamp_fusion), kind=kCustom, calls=%fused_computation | custom fusion | bytes 98304 | tf_op jit(solution)/shard_map/jit(_take)/gather | solution.py:95
  83.2 0.1 convert_reduce_fusion.1
  83.3 136.5 %all-to-all-done = bf16[4,32,64,512]{3,2,1,0:T(8,128)(2,1)} async-done(((bf16[4,32,64,512]{3,2,1,0:T(8,128)(2,1)}), bf16[4,32,64,512]{3,2,1,0:T(8,128)(2,1)}, u32[]{:S(2)}, u32[]{:S(2)}) %all-to-all-start) | async-done | bytes 8388640 | tf_op jit(solution)/shard_map/all_to_all | solution.py:78
  219.9 0.0 copy-done.3
  219.9 0.0 copy-start.4
  219.9 18.0 %fusion = (f32[1024]{0:T(1024)S(1)}, f32[8192,1024]{1,0:T(8,128)}) fusion(s32[1024]{0:T(1024)S(1)} %convert_reduce_fusion.1, s32[8192]{0:T(1024)S(1)} %eq.147, bf16[8192,512]{1,0:T(8,128)(2,1)} %bitcast.8, bf16[1024,512]{1,0:T(8,128)(2,1)S(1)} %copy-done.3), kind=kOutput, calls=%fused_computation.11 | convolution fusion | flops 8623488000 | bytes 43032576 | tf_op jit(solution)/shard_map/dot_general | solution.py:108
  237.9 4.9 %pmax.7 = f32[1024]{0:T(1024)S(1)} all-reduce(f32[1024]{0:T(1024)S(1)} %get-tuple-element.214), channel_id=1, replica_groups=mesh['groups'=2,'pack'=4,'mp'=2,'sub'=2] {'mp'}, use_global_device_ids=true, to_apply=%region_7.8 | all-reduce | flops 1024 | bytes 8192 | tf_op jit(solution)/shard_map/pmax | solution.py:117
  242.8 0.0 copy-done.4
  242.8 18.5 %fusion.10 = (f32[1024]{0:T(1024)S(1)}, f32[1024]{0:T(1024)S(1)}) fusion(f32[1024]{0:T(1024)S(1)} %pmax.7, f32[8192,1024]{1,0:T(8,128)} %get-tuple-element.215, s32[8192]{0:T(1024)S(1)} %eq.147, s32[1024]{0:T(1024)S(1)} %convert_reduce_fusion.1, s32[1024]{0:T(1024)S(1)} %copy-done.4, s32[8192]{0:T(1024)S(1)} %and_select_fusion.2), kind=kLoop, calls=%fused_computation.63 | loop fusion | flops 83884032 | bytes 33640448 | tf_op jit(solution)/shard_map/reduce_sum | solution.py:120
  261.3 5.0 %all-reduce = (f32[1024]{0:T(1024)S(1)}, f32[1024]{0:T(1024)S(1)}) all-reduce(f32[1024]{0:T(1024)S(1)} %get-tuple-element.187, f32[1024]{0:T(1024)S(1)} %get-tuple-element.186), channel_id=1, replica_groups=mesh['groups'=2,'pack'=4,'mp'=2,'sub'=2] {'mp'}, use_global_device_ids=true, to_apply=%region_19.20 | all-reduce | flops 2048 | bytes 16384 | tf_op jit(solution)/shard_map/psum | solution.py:119
  266.3 23.6 %fusion.1 = f32[1024,512]{1,0:T(8,128)} fusion(bf16[8192,512]{1,0:T(8,128)(2,1)} %bitcast.8, f32[1024]{0:T(1024)S(1)} %get-tuple-element.207, f32[8192,1024]{1,0:T(8,128)} %get-tuple-element.215, f32[1024]{0:T(1024)S(1)} %pmax.7, s32[1024]{0:T(1024)S(1)} %convert_reduce_fusion.1, s32[8192]{0:T(1024)S(1)} %eq.147), kind=kOutput, calls=%fused_computation.12 | convolution fusion | flops 8648654848 | bytes 44085248 | tf_op jit(solution)/shard_map/dot_general | solution.py:123
  289.8 0.0 all-reduce.3.cloned.1.call-update
  289.9 0.0 copy-start.1
  289.9 0.0 copy-start.5
  289.9 62.2 %all-reduce.3.cloned.1.call-done = f32[1024,512]{1,0:T(8,128)} async-done(((f32[1024,512]{1,0:T(8,128)}), f32[1024,512]{1,0:T(8,128)}) %all-reduce.3.cloned.1.call-update) | async-done | bytes 2097168 | tf_op jit(solution)/shard_map/psum | solution.py:124
  352.1 3.2 fusion.11
  355.3 1.4 select_reduce_fusion.1
  356.7 5.2 %all-gather.1 = f32[4096]{0:T(1024)S(1)} all-gather(f32[1024]{0:T(1024)S(1)} %get-tuple-element.189), channel_id=3, replica_groups=mesh['groups'=2,'pack'=4,'mp'=2,'sub'=2] {'mp','sub'}, dimensions={0}, use_global_device_ids=true | all-gather | bytes 20480 | tf_op jit(solution)/shard_map/all_gather | solution.py:16
  361.9 5.2 %all-gather.2 = f32[4096]{0:T(1024)S(1)} all-gather(f32[1024]{0:T(1024)S(1)} %get-tuple-element.188), channel_id=4, replica_groups=mesh['groups'=2,'pack'=4,'mp'=2,'sub'=2] {'mp','sub'}, dimensions={0}, use_global_device_ids=true | all-gather | bytes 20480 | tf_op jit(solution)/shard_map/all_gather | solution.py:16
  367.1 5.2 %all-gather = f32[4096]{0:T(1024)S(1)} all-gather(f32[1024]{0:T(1024)S(1)} %get-tuple-element.216), channel_id=2, replica_groups=mesh['groups'=2,'pack'=4,'mp'=2,'sub'=2] {'mp','sub'}, dimensions={0}, use_global_device_ids=true | all-gather | bytes 20480 | tf_op jit(solution)/shard_map/all_gather | solution.py:16
  372.3 0.3 while.19
  372.6 0.0 copy-done.5
  372.6 2.0 multiply_reduce_fusion
  374.6 0.6 log_negate_fusion
  375.3 0.0 copy-done.1
  (31 shorter events, 0.3 us)
Async XLA Ops:
  6.5 1.6 copy-start
  29.3 8.1 %copy-start.6 = (s32[1,4]{1,0:T(1,128)S(1)}, s32[1,4]{1,0:T(1,128)}, u32[]{:S(2)}) copy-start(s32[1,4]{1,0:T(1,128)} %param.18) | copy-start | bytes 52
  29.3 8.3 %copy-start.2 = (s32[8192]{0:T(1024)S(1)}, s32[8192]{0:T(1024)}, u32[]{:S(2)}) copy-start(s32[8192]{0:T(1024)} %param.16) | copy-start | bytes 98308
  29.3 190.5 %all-to-all-start = ((bf16[4,32,64,512]{3,2,1,0:T(8,128)(2,1)}), bf16[4,32,64,512]{3,2,1,0:T(8,128)(2,1)}, u32[]{:S(2)}, u32[]{:S(2)}) async-start(bf16[4,32,64,512]{3,2,1,0:T(8,128)(2,1)} %bitcast.44), calls=%async_computation | async-start | bytes 16777216 | tf_op jit(solution)/shard_map/all_to_all | solution.py:78
  35.8 316.3 %all-reduce.3.cloned.1.call-start = ((), (), s32[]{:S(2)}) async-start(), calls=%async_computation.1 | async-start | bytes 4194304 | tf_op jit(solution)/shard_map/psum | solution.py:124
  37.7 182.2 %copy-start.3 = (bf16[1024,512]{1,0:T(8,128)(2,1)S(1)}, bf16[1024,512]{1,0:T(8,128)(2,1)}, u32[]{:S(2)}) copy-start(bf16[1024,512]{1,0:T(8,128)(2,1)} %param.11) | copy-start | bytes 3145732
  219.9 22.9 %copy-start.4 = (s32[1024]{0:T(1024)S(1)}, s32[1024]{0:T(1024)}, u32[]{:S(2)}) copy-start(s32[1024]{0:T(1024)} %param.19) | copy-start | bytes 12292
  289.9 85.4 %copy-start.1 = (bf16[1024,1024]{1,0:T(8,128)(2,1)S(1)}, bf16[1024,1024]{1,0:T(8,128)(2,1)}, u32[]{:S(2)}) copy-start(bf16[1024,1024]{1,0:T(8,128)(2,1)} %param.12) | copy-start | bytes 6291460
  289.9 82.7 %copy-start.5 = (f32[512]{0:T(512)S(1)}, f32[512]{0:T(512)}, u32[]{:S(2)}) copy-start(f32[512]{0:T(512)} %param.15) | copy-start | bytes 6148
Sparse Core Ops, SparseCore 0:
  290.0 62.0 all-reduce.2
where the time goes:
time: 383 us; the launch traced here: 382 us
  waiting for transfers between devices  199 us (52%)
  local copies, waits for them, and re-layouts  57.4 us (15%)
  matrix products  52.7 us (14%)
  other arithmetic  27.5 us (7%)
  blocking collectives  25.5 us (7%)
  between operations  13.6 us (4%)
  starting transfers between devices  6.46 us (2%)
    all_to_all x1, waiting for transfers between devices, per_device(): lax.all_to_all(outgoing, 'pack', split_axis=0, concat_axis=0, tiled=True)  137 us
    psum x1, waiting for transfers between devices, per_device(): context = lax.psum(partial_value, 'mp')  62.2 us
    gather x1, local copies, waits for them, and re-layouts, per_device(): jnp.take(phrase_token, (slot_block[:, :, None] * BLK + jnp.arange(BLK, dt...  45.5 us
    dot_general x1, matrix products, per_device(): jnp.dot(weights, slot_keys, preferred_element_type=jnp.float32)  23.6 us
    reduce_sum x1, other arithmetic, per_device(): jnp.sum(row_exp, axis=1)  18.5 us
    dot_general x1, matrix products, per_device(): lax.dot_general(frame_enc, slot_keys, (((1,), (1,)), ((), ())), preferred...  18 us
    all_gather x3, blocking collectives, joined(): everything = jax.tree.map(lambda part: lax.all_gather(part, axis), shard)  15.6 us
    unnamed x15, local copies, waits for them, and re-layouts  10.2 us
  transfers between devices with their start and end apart: 2, of which 2 were waited for; matrix products, arithmetic and copies ran while one was open for 12% of the time, Pallas kernels for 0%

commit v1 on v0

v1 whole, which is shorter than its diff:
```python
import functools
import math

import jax
import jax.numpy as jnp
from jax import lax
from jax.experimental import pallas as pl
from jax.experimental.pallas import tpu as pltpu
from jax.sharding import PartitionSpec as P

BLK = 64
MESH = pl.DeviceIdType.MESH
GAIN = 2.0
HIDDEN_LOW = -1e30
FLOOR = -1e25
F32 = jnp.float32
BF16 = jnp.bfloat16
PIECES = 2
ROWS = 256


def eye(n):
    return lax.broadcasted_iota(jnp.int32, (n, n), 0) == lax.broadcasted_iota(jnp.int32, (n, n), 1)


def to_row(col):
    return jnp.sum(jnp.where(eye(col.shape[0]), col, 0.0), axis=0, keepdims=True)


def to_col(row):
    return jnp.sum(jnp.where(eye(row.shape[1]), row, 0.0), axis=1, keepdims=True)


def lane_sum(x):
    total = x[:, :128]
    for i in range(1, x.shape[1] // 128):
        total = total + x[:, i * 128 : (i + 1) * 128]
    return total


def kernel(
    dims,
    frame_hbm, phrase_hbm, kw_hbm, ow_hbm, gw_ref, tok_ref, list_ref, utt_ref, tgt_ref,
    out_ref,
    frames, phrase, kw, keys, ow_all, tcol, bcol, m_ref, l_ref, p_ref, acc,
    c1_send, c1_recv, s1_send, s1_recv, c2_send, c2_recv, s2_send, s2_recv, hid, st3,
    load_sem, rs, rr, ls, lr, ow_s, ow_r, x1_s, x1_r, x2_s, x2_r, h_s, h_r, t_s, t_r,
):
    packs, mp, sub, lanes = dims
    z, x, c = lax.axis_index("pack"), lax.axis_index("mp"), lax.axis_index("sub")
    plane = mp * sub
    me = x * sub + c
    other = 1 - c
    fr, width = frames.shape
    own_half = phrase.shape[0]
    ph = own_half // PIECES
    half = fr // sub
    part = half // mp
    vcols = ow_hbm.shape[1]
    utts = utt_ref.shape[1]
    entries = list_ref.shape[1]
    per_utt = entries // utts
    half_blocks = own_half // BLK
    scale = GAIN / math.sqrt(width)

    barrier = pltpu.get_barrier_semaphore()

    @pl.when(z > 0)
    def _():
        pl.semaphore_signal(barrier, inc=1, device_id={"pack": z - 1}, device_id_type=MESH)

    @pl.when(z + 1 < packs)
    def _():
        pl.semaphore_signal(barrier, inc=1, device_id={"pack": z + 1}, device_id_type=MESH)

    def peer(j):
        d = lax.rem(me + j, plane)
        return {"mp": d // sub, "sub": lax.rem(d, sub)}

    for j in range(1, plane):
        pl.semaphore_signal(barrier, inc=1, device_id=peer(j), device_id_type=MESH)

    loads = [
        pltpu.make_async_copy(phrase_hbm.at[pl.ds(c * own_half, own_half), :], phrase, load_sem.at[0]),
        pltpu.make_async_copy(kw_hbm, kw, load_sem.at[1]),
        pltpu.make_async_copy(frame_hbm, frames, load_sem.at[2]),
        pltpu.make_async_copy(ow_hbm, ow_all.at[x], load_sem.at[3]),
    ]
    for load in loads:
        load.start()

    def right(s, origin):
        piece = keys.at[origin, pl.ds(lax.rem(s, PIECES) * ph, ph), :]
        return pltpu.make_async_remote_copy(
            src_ref=piece, dst_ref=piece, send_sem=rs.at[s], recv_sem=rr.at[s],
            device_id={"pack": lax.min(z + 1, packs - 1)}, device_id_type=MESH,
        )

    def left(s, origin):
        piece = keys.at[origin, pl.ds(lax.rem(s, PIECES) * ph, ph), :]
        return pltpu.make_async_remote_copy(
            src_ref=piece, dst_ref=piece, send_sem=ls.at[s], recv_sem=lr.at[s],
            device_id={"pack": lax.max(z - 1, 0)}, device_id_type=MESH,
        )

    loads[0].wait()
    loads[1].wait()
    ends_n = jnp.where(z > 0, 1, 0) + jnp.where(z + 1 < packs, 1, 0)
    pl.semaphore_wait(barrier, ends_n + (plane - 1))

    def project(h, carry):
        rows = pl.ds(h * ph, ph)
        keys[z, rows, :] = jnp.dot(phrase[rows, :], kw[...], preferred_element_type=F32).astype(BF16)

        @pl.when(z + 1 < packs)
        def _():
            right(h, z).start()

        @pl.when(z > 0)
        def _():
            left(h, z).start()

        return carry

    lax.fori_loop(0, PIECES, project, 0)

    loads[2].wait()
    loads[3].wait()

    def ow_copy(j, slot):
        return pltpu.make_async_remote_copy(
            src_ref=ow_all.at[slot], dst_ref=ow_all.at[slot], send_sem=ow_s.at[j - 1], recv_sem=ow_r.at[j - 1],
            device_id={"mp": lax.rem(x + j, mp)}, device_id_type=MESH,
        )

    for j in range(1, mp):
        ow_copy(j, x).start()

    for i in range(fr // 128):
        tcol[i * 128 : (i + 1) * 128, :] = to_col(tgt_ref[i : i + 1, :].astype(F32))
    bcol[...] = to_col(list_ref[pl.ds(z, 1), :].astype(F32))
    m_ref[...] = jnp.full(m_ref.shape, FLOOR, F32)
    l_ref[...] = jnp.zeros(l_ref.shape, F32)
    p_ref[...] = jnp.zeros(p_ref.shape, F32)
    acc[...] = jnp.zeros(acc.shape, F32)
    ends = []
    so_far = 0
    for u in range(utts):
        so_far = so_far + utt_ref[0, u]
        ends.append(so_far)

    def process(origin, h):
        k = keys[origin, pl.ds(h * ph, ph), :]
        block = (origin * mp + x) * (half_blocks * sub) + c * half_blocks + h * (ph // BLK)
        ids = (block + lax.broadcasted_iota(jnp.int32, (1, ph), 1) // BLK).astype(F32)
        listed = jnp.where(bcol[...] == ids, 1.0, 0.0)
        log_count = []
        for u in range(utts):
            count = jnp.sum(listed[u * per_utt : (u + 1) * per_utt, :], axis=0, keepdims=True)
            log_count.append(jnp.where(count > 0.5, jnp.log(jnp.maximum(count, 1.0)), HIDDEN_LOW))
        tok_first = block * BLK // 128
        tokens = jnp.concatenate(
            [tok_ref[pl.ds(tok_first + i, 1), :] for i in range(ph // 128)], axis=1
        ).astype(F32)

        def rows_step(i, carry):
            rows = pl.ds(i * ROWS, ROWS)
            s = lax.dot_general(frames[rows, :], k, (((1,), (1,)), ((), ())), preferred_element_type=F32)
            frame_id = lax.broadcasted_iota(jnp.int32, (ROWS, ph), 0) + i * ROWS
            bias = jnp.broadcast_to(log_count[utts - 1], (ROWS, ph))
            for u in range(utts - 2, -1, -1):
                bias = jnp.where(frame_id < ends[u], log_count[u], bias)
            s = s * scale + bias
            old = m_ref[rows, :]
            new = jnp.maximum(old, jnp.max(s, axis=1, keepdims=True))
            fade = jnp.exp(old - new)
            e = jnp.exp(s - new)
            hits = jnp.where(tokens == tcol[rows, :], e, 0.0)
            m_ref[rows, :] = new
            l_ref[rows, :] = l_ref[rows, :] * fade + lane_sum(e)
            p_ref[rows, :] = p_ref[rows, :] * fade + lane_sum(hits)
            acc[rows, :] = acc[rows, :] * fade + jnp.dot(e.astype(BF16), k, preferred_element_type=F32)
            return carry

        lax.fori_loop(0, fr // ROWS, rows_step, 0)

    def own_step(h, carry):
        process(z, h)
        return carry

    lax.fori_loop(0, PIECES, own_step, 0)

    def gather_step(s, carry):
        t, h = s // PIECES, lax.rem(s, PIECES)
        from_left, from_right = z - 1 - t, z + 1 + t

        @pl.when(from_left >= 0)
        def _():
            right(s, from_left).wait_recv()

            @pl.when(z + 1 < packs)
            def _():
                right(s + PIECES, from_left).start()

        @pl.when(from_right < packs)
        def _():
            left(s, from_right).wait_recv()

            @pl.when(z > 0)
            def _():
                left(s + PIECES, from_right).start()

        @pl.when(from_left >= 0)
        def _():
            process(from_left, h)

        @pl.when(from_right < packs)
        def _():
            process(from_right, h)

        return carry

    lax.fori_loop(0, (packs - 1) * PIECES, gather_step, 0)

    blocks = half // lanes
    for i in range(blocks):
        rows = pl.ds(other * half + i * lanes, lanes)
        c1_send[i * lanes : (i + 1) * lanes, :] = acc[rows, :].astype(BF16)
        s1_send[0, i : i + 1, :] = to_row(m_ref[rows, :])
        s1_send[1, i : i + 1, :] = to_row(jnp.sum(l_ref[rows, :], axis=1, keepdims=True))
        s1_send[2, i : i + 1, :] = to_row(jnp.sum(p_ref[rows, :], axis=1, keepdims=True))

    def to_other(src, dst, send, recv):
        return pltpu.make_async_remote_copy(
            src_ref=src, dst_ref=dst, send_sem=send, recv_sem=recv,
            device_id={"sub": other}, device_id_type=MESH,
        )

    first = [
        to_other(c1_send, c1_recv, x1_s.at[0], x1_r.at[0]),
        to_other(s1_send, s1_recv, x1_s.at[1], x1_r.at[1]),
    ]
    for copy in first:
        copy.start()
    for copy in first:
        copy.wait_recv()

    def merge(rows, total, pointer, more, stats):
        old = m_ref[rows, :]
        theirs = to_col(stats[0])
        new = jnp.maximum(old, theirs)
        a, b = jnp.exp(old - new), jnp.exp(theirs - new)
        m_ref[rows, :] = new
        total = total * a + to_col(stats[1]) * b
        pointer = pointer * a + to_col(stats[2]) * b
        acc[rows, :] = acc[rows, :] * a + more.astype(F32) * b
        return total, pointer

    def second(j):
        return [
            pltpu.make_async_remote_copy(
                src_ref=a.at[j - 1], dst_ref=b.at[j - 1],
                send_sem=x2_s.at[2 * (j - 1) + k], recv_sem=x2_r.at[2 * (j - 1) + k],
                device_id={"mp": lax.rem(x + j, mp)}, device_id_type=MESH,
            )
            for k, (a, b) in enumerate(((c2_send, c2_recv), (s2_send, s2_recv)))
        ]

    per = part // lanes
    own_totals = []
    for j in list(range(1, mp)) + [0]:
        target = lax.rem(x + j, mp)
        for i in range(per):
            at = target * part + i * lanes
            rows = pl.ds(c * half + at, lanes)
            spot = target * per + i
            total, pointer = merge(
                rows,
                jnp.sum(l_ref[rows, :], axis=1, keepdims=True),
                jnp.sum(p_ref[rows, :], axis=1, keepdims=True),
                c1_recv[pl.ds(at, lanes), :],
                [s1_recv[k, pl.ds(spot, 1), :] for k in range(3)],
            )
            if j == 0:
                own_totals.append((total, pointer))
            else:
                c2_send[j - 1, i * lanes : (i + 1) * lanes, :] = acc[rows, :].astype(BF16)
                s2_send[j - 1, 0, i : i + 1, :] = to_row(m_ref[rows, :])
                s2_send[j - 1, 1, i : i + 1, :] = to_row(total)
                s2_send[j - 1, 2, i : i + 1, :] = to_row(pointer)
        if j > 0:
            for copy in second(j):
                copy.start()
    for j in range(1, mp):
        for copy in second(j):
            copy.wait_recv()
    own_first = c * half + x * part
    for i in range(per):
        rows = pl.ds(own_first + i * lanes, lanes)
        total, pointer = own_totals[i]
        for j in range(1, mp):
            total, pointer = merge(
                rows, total, pointer,
                c2_recv[j - 1, i * lanes : (i + 1) * lanes, :],
                [s2_recv[j - 1, k, i : i + 1, :] for k in range(3)],
            )
        hidden = jnp.tanh(frames[rows, :].astype(F32) + acc[rows, :] / total).astype(BF16)
        hid[pl.ds(c * part + i * lanes, lanes), :] = hidden
        gate = jnp.sum(hidden.astype(F32) * gw_ref[...], axis=1, keepdims=True)
        st3[me, 3 * sub, i : i + 1, :] = to_row(gate)
        st3[me, 3 * sub + 1, i : i + 1, :] = to_row(pointer / total)

    mine = hid.at[pl.ds(c * part, part), :]
    hid_copy = to_other(mine, mine, h_s, h_r)
    hid_copy.start()
    for j in range(1, mp):
        ow_copy(j, lax.rem(x + mp - j, mp)).wait_recv()

    chunk = min(512, vcols)

    def vocabulary(g):
        h = hid[pl.ds(g * part, part), :]
        target = tcol[pl.ds(g * half + x * part, part), :]
        top = jnp.full((part, 128), FLOOR, F32)
        total = jnp.zeros((part, 128), F32)
        chosen = jnp.zeros((part, 128), F32)
        for q in range(mp):
            for v in range(vcols // chunk):
                w = ow_all[q, :, v * chunk : (v + 1) * chunk]
                logits = jnp.dot(h, w, preferred_element_type=F32)
                first_col = (q * sub + c) * vcols + v * chunk
                ids = (lax.broadcasted_iota(jnp.int32, (1, chunk), 1) + first_col).astype(F32)
                chosen = chosen + lane_sum(jnp.where(ids == target, logits, 0.0))
                new = top
                for i in range(chunk // 128):
                    new = jnp.maximum(new, logits[:, i * 128 : (i + 1) * 128])
                total = total * jnp.exp(top - new)
                for i in range(chunk // 128):
                    total = total + jnp.exp(logits[:, i * 128 : (i + 1) * 128] - new)
                top = new
        row_top = jnp.max(top, axis=1, keepdims=True)
        row_sum = jnp.sum(total * jnp.exp(top - row_top), axis=1, keepdims=True)
        row_hit = jnp.sum(chosen, axis=1, keepdims=True)
        for i in range(per):
            cut = slice(i * lanes, (i + 1) * lanes)
            st3[me, g * 3, i : i + 1, :] = to_row(row_top[cut])
            st3[me, g * 3 + 1, i : i + 1, :] = to_row(row_sum[cut])
            st3[me, g * 3 + 2, i : i + 1, :] = to_row(row_hit[cut])

    vocabulary(c)
    to_other(mine, hid.at[pl.ds(other * part, part), :], h_s, h_r).wait_recv()
    vocabulary(other)

    def share(j, slot):
        return pltpu.make_async_remote_copy(
            src_ref=st3.at[slot], dst_ref=st3.at[slot], send_sem=t_s.at[j - 1], recv_sem=t_r.at[j - 1],
            device_id=peer(j), device_id_type=MESH,
        )

    for j in range(1, plane):
        share(j, me).start()
    for j in range(1, plane):
        share(j, lax.rem(me + plane - j, plane)).wait_recv()

    for q in range(mp):
        for g in range(sub):
            one, two = q * sub, q * sub + 1
            top_a, top_b = st3[one, g * 3], st3[two, g * 3]
            top = jnp.maximum(top_a, top_b)
            total = st3[one, g * 3 + 1] * jnp.exp(top_a - top) + st3[two, g * 3 + 1] * jnp.exp(top_b - top)
            log_norm = top + jnp.log(total)
            hit = st3[one, g * 3 + 2] + st3[two, g * 3 + 2]
            gate = 1.0 / (1.0 + jnp.exp(-st3[q * sub + g, 3 * sub]))
            mixed = (1.0 - gate) * jnp.exp(hit - log_norm) + gate * st3[q * sub + g, 3 * sub + 1]
            first_row = (g * mp + q) * per
            out_ref[first_row : first_row + per, :] = -jnp.log(mixed)

    def send_waits(s, carry):
        t = s // PIECES

        @pl.when((z >= t) & (z + 1 < packs))
        def _():
            right(s, z - t).wait_send()

        @pl.when((z + t < packs) & (z > 0))
        def _():
            left(s, z + t).wait_send()

        return carry

    lax.fori_loop(0, (packs - 1) * PIECES, send_waits, 0)
    for copy in first:
        copy.wait_send()
    hid_copy.wait_send()
    for j in range(1, mp):
        ow_copy(j, x).wait_send()
        for copy in second(j):
            copy.wait_send()
    for j in range(1, plane):
        share(j, me).wait_send()


def per_device(
    frame_enc, phrase_enc, key_weight, out_weight, gate_weight,
    phrase_token, bias_blocks, utt_lengths, targets,
):
    packs = lax.axis_size("pack")
    mp = lax.axis_size("mp")
    sub = lax.axis_size("sub")
    plane = mp * sub
    fr, width = frame_enc.shape
    depth = phrase_enc.shape[1]
    own_half = phrase_enc.shape[0] // sub
    vcols = out_weight.shape[1]
    half = fr // sub
    part = half // mp
    lanes = min(part, 128)
    entries = bias_blocks.shape[1]
    hops = (packs - 1) * PIECES
    others = max(mp - 1, 1)
    vmem = pltpu.VMEM
    dma = pltpu.SemaphoreType.DMA
    any_spec = pl.BlockSpec(memory_space=pl.ANY)
    vmem_spec = pl.BlockSpec(memory_space=vmem)
    smem_spec = pl.BlockSpec(memory_space=pltpu.SMEM)
    out = pl.pallas_call(
        functools.partial(kernel, (packs, mp, sub, lanes)),
        out_shape=jax.ShapeDtypeStruct((fr // lanes, lanes), F32),
        in_specs=[any_spec] * 4 + [vmem_spec] * 3 + [smem_spec, vmem_spec],
        out_specs=vmem_spec,
        scratch_shapes=[
            vmem((fr, width), BF16),
            vmem((own_half, depth), BF16),
            vmem((depth, width), BF16),
            vmem((packs, own_half, width), BF16),
            vmem((mp, width, vcols), BF16),
            vmem((fr, 1), F32),
            vmem((entries, 1), F32),
            vmem((fr, 1), F32),
            vmem((fr, 128), F32),
            vmem((fr, 128), F32),
            vmem((fr, width), F32),
            vmem((half, width), BF16),
            vmem((half, width), BF16),
            vmem((3, half // lanes, lanes), F32),
            vmem((3, half // lanes, lanes), F32),
            vmem((others, part, width), BF16),
            vmem((others, part, width), BF16),
            vmem((others, 3, part // lanes, lanes), F32),
            vmem((others, 3, part // lanes, lanes), F32),
            vmem((sub * part, width), BF16),
            vmem((plane, 3 * sub + 2, part // lanes, lanes), F32),
            dma((4,)), dma((hops,)), dma((hops,)), dma((hops,)), dma((hops,)),
            dma((others,)), dma((others,)), dma((2,)), dma((2,)),
            dma((2 * others,)), dma((2 * others,)), dma, dma,
            dma((plane - 1,)), dma((plane - 1,)),
        ],
        compiler_params=pltpu.CompilerParams(
            collective_id=0, has_side_effects=True, vmem_limit_bytes=56 * 1024 * 1024
        ),
    )(
        frame_enc, phrase_enc, key_weight, out_weight,
        gate_weight.reshape(1, width),
        phrase_token.reshape(-1, 128),
        bias_blocks, utt_lengths,
        targets.reshape(-1, 128),
    )
    return out.reshape(fr)


def solution(mesh):
    in_specs = (
        P(("groups", "pack"), None),
        P(("groups", "pack", "mp"), None),
        P(),
        P(None, ("mp", "sub")),
        P(),
        P("groups"),
        P("groups", None),
        P(("groups", "pack"), None),
        P(("groups", "pack")),
    )
    return jax.shard_map(
        per_device, mesh=mesh, in_specs=in_specs, out_specs=P(("groups", "pack")), check_vma=False
    )
```

time: 383 us -> 61.5 us (0.16)
  waiting for transfers between devices: 199 us -> 0 us
  Pallas kernels: 0 us -> 60.1 us
  local copies, waits for them, and re-layouts: 57.4 us -> 1.28 us
  matrix products: 52.7 us -> 0 us
  other arithmetic: 27.5 us -> 0 us
  blocking collectives: 25.5 us -> 0 us
  between operations: 13.6 us -> 0.01 us
  starting transfers between devices: 6.46 us -> 0 us
    all_to_all x1 -> x0, waiting for transfers between devices: 137 us -> none  [per_device(): lax.all_to_all(outgoing, 'pack', split_axis=0, concat_axis=0, tiled=True)]
    psum x1 -> x0, waiting for transfers between devices: 62.2 us -> none  [per_device(): context = lax.psum(partial_value, 'mp')]
    pallas_call x0 -> x1, Pallas kernels: none -> 60.1 us  [per_device(): pl.pallas_call(functools.partial(kernel, (packs, mp, sub, lanes)), out_sh...]
    dot_general x5 -> x0, matrix products: 52.7 us -> none  [the longest x1 23.6 us: per_device(): jnp.dot(weights, slot_keys, preferred_element_type=jnp.float32)]
    gather x1 -> x0, local copies, waits for them, and re-layouts: 45.5 us -> none  [per_device(): jnp.take(phrase_token, (slot_block[:, :, None] * BLK + jnp.arange(BLK, dt...]
    reduce_sum x6 -> x0, other arithmetic: 22.4 us -> none  [the longest x1 18.5 us: per_device(): jnp.sum(row_exp, axis=1)]
    all_gather x3 -> x0, blocking collectives: 15.6 us -> none  [joined(): everything = jax.tree.map(lambda part: lax.all_gather(part, axis), shard)]
    unnamed x15 -> x1, local copies, waits for them, and re-layouts: 10.2 us -> 1.28 us
  transfers between devices with their start and end apart: 2 -> 0, of which waited for: 2 -> 0; matrix products, arithmetic and copies ran while one was open for 12% -> 0% of each run, Pallas kernels for 0% -> 0%
where the time goes in v1:
time: 61.5 us; the launch traced here: 61.3 us
  Pallas kernels  60.1 us (98%)
  local copies, waits for them, and re-layouts  1.28 us (2%)
    pallas_call x1, Pallas kernels, per_device(): pl.pallas_call(functools.partial(kernel, (packs, mp, sub, lanes)), out_sh...  60.1 us
    unnamed x1, local copies, waits for them, and re-layouts  1.28 us

profile of v1, /device:TPU:0, one launch (start us, length us, event | category | flops | bytes accessed | tf_op | source)
XLA Modules:
  0.0 61.3 jit_solution(11139490244842354048)
XLA Ops:
  0.0 60.1 %shard_map.91 = f32[8,128]{1,0:T(8,128)} custom-call(bf16[1024,512]{1,0:T(8,128)(2,1)} %frame_hbm.1, bf16[1024,1024]{1,0:T(8,128)(2,1)} %phrase_hbm.1, bf16[1024,512]{1,0:T(8,128)(2,1)} %kw_hbm.1, bf16[512,1024]{1,0:T(8,128)(2,1)} %ow_hbm.1, f32[1,512]{1,0:T(1,128)} %bitcast.7, s32[64,128]{1,0:T(8,128)} %bitcast.4, s32[4,128]{1,0:T(4,128)} %list_ref.1, ...), custom_call_target="tpu_custom_call" | custom-call | tf_op jit(solution)/shard_map/pallas_call | solution.py:426
  60.1 1.3 %copy.11 = f32[1024]{0:T(1024)} copy(f32[1024]{0:T(1024)} %bitcast.5) | data formatting | bytes 8192

commit v2 on v1

v2 whole, which is shorter than its diff:
```python
import functools
import math

import jax
import jax.numpy as jnp
from jax import lax
from jax.experimental import pallas as pl
from jax.experimental.pallas import tpu as pltpu
from jax.sharding import PartitionSpec as P

BLK = 64
MESH = pl.DeviceIdType.MESH
GAIN = 2.0
HIDDEN_LOW = -1e30
FLOOR = -1e25
F32 = jnp.float32
BF16 = jnp.bfloat16
PIECES = 4
ROWS = 256


def eye(n):
    return lax.broadcasted_iota(jnp.int32, (n, n), 0) == lax.broadcasted_iota(jnp.int32, (n, n), 1)


def to_row(col):
    return jnp.sum(jnp.where(eye(col.shape[0]), col, 0.0), axis=0, keepdims=True)


def to_col(row):
    return jnp.sum(jnp.where(eye(row.shape[1]), row, 0.0), axis=1, keepdims=True)


def lane_sum(x):
    total = x[:, :128]
    for i in range(1, x.shape[1] // 128):
        total = total + x[:, i * 128 : (i + 1) * 128]
    return total


def kernel(
    dims,
    frame_hbm, phrase_hbm, kw_hbm, ow_hbm, gw_ref, tok_ref, list_ref, utt_ref, tgt_ref,
    out_ref,
    frames, phrase, kw, keys, ow_all, tcol, bcol, m_ref, l_ref, p_ref, acc,
    c2_send, c2_recv, s2_send, s2_recv, hid, st3,
    load_sem, rs, rr, ls, lr, cs, cr, ow_s, ow_r, x2_s, x2_r, h_s, h_r, t_s, t_r,
):
    packs, mp, sub, lanes = dims
    z, x, c = lax.axis_index("pack"), lax.axis_index("mp"), lax.axis_index("sub")
    plane = mp * sub
    me = x * sub + c
    other = 1 - c
    half, width = frames.shape
    own_half = phrase.shape[0]
    ph = own_half // PIECES
    both = sub * ph
    part = half // mp
    vcols = ow_hbm.shape[1]
    utts = utt_ref.shape[1]
    entries = list_ref.shape[1]
    per_utt = entries // utts
    half_blocks = own_half // BLK
    scale = GAIN / math.sqrt(width)
    per = part // lanes
    step_rows = min(ROWS, part)

    barrier = pltpu.get_barrier_semaphore()

    @pl.when(z > 0)
    def _():
        pl.semaphore_signal(barrier, inc=1, device_id={"pack": z - 1}, device_id_type=MESH)

    @pl.when(z + 1 < packs)
    def _():
        pl.semaphore_signal(barrier, inc=1, device_id={"pack": z + 1}, device_id_type=MESH)

    def peer(j):
        d = lax.rem(me + j, plane)
        return {"mp": d // sub, "sub": lax.rem(d, sub)}

    for j in range(1, plane):
        pl.semaphore_signal(barrier, inc=1, device_id=peer(j), device_id_type=MESH)

    def phrase_load(h):
        return pltpu.make_async_copy(
            phrase_hbm.at[pl.ds(c * own_half + h * ph, ph), :], phrase.at[pl.ds(h * ph, ph), :], load_sem.at[3 + h]
        )

    loads = [
        pltpu.make_async_copy(kw_hbm, kw, load_sem.at[0]),
        pltpu.make_async_copy(frame_hbm.at[pl.ds(c * half, half), :], frames, load_sem.at[1]),
        pltpu.make_async_copy(ow_hbm, ow_all.at[x], load_sem.at[2]),
    ]
    loads[0].start()
    for h in range(PIECES):
        phrase_load(h).start()
    loads[2].start()
    loads[1].start()

    def right(s, origin):
        piece = keys.at[origin, lax.rem(s, PIECES), c]
        return pltpu.make_async_remote_copy(
            src_ref=piece, dst_ref=piece, send_sem=rs.at[s], recv_sem=rr.at[s],
            device_id={"pack": lax.min(z + 1, packs - 1)}, device_id_type=MESH,
        )

    def left(s, origin):
        piece = keys.at[origin, lax.rem(s, PIECES), c]
        return pltpu.make_async_remote_copy(
            src_ref=piece, dst_ref=piece, send_sem=ls.at[s], recv_sem=lr.at[s],
            device_id={"pack": lax.max(z - 1, 0)}, device_id_type=MESH,
        )

    def to_other(src, dst, send, recv):
        return pltpu.make_async_remote_copy(
            src_ref=src, dst_ref=dst, send_sem=send, recv_sem=recv,
            device_id={"sub": other}, device_id_type=MESH,
        )

    def across(origin, h, core):
        piece = keys.at[origin, h, core]
        spot = origin * PIECES + h
        return to_other(piece, piece, cs.at[spot], cr.at[spot])

    ends_n = jnp.where(z > 0, 1, 0) + jnp.where(z + 1 < packs, 1, 0)
    pl.semaphore_wait(barrier, ends_n + (plane - 1))
    loads[0].wait()

    def project(h, carry):
        phrase_load(h).wait()
        rows = pl.ds(h * ph, ph)
        keys[z, h, c] = jnp.dot(phrase[rows, :], kw[...], preferred_element_type=F32).astype(BF16)

        @pl.when(z + 1 < packs)
        def _():
            right(h, z).start()

        @pl.when(z > 0)
        def _():
            left(h, z).start()

        across(z, h, c).start()
        return carry

    lax.fori_loop(0, PIECES, project, 0)

    loads[2].wait()

    def ow_copy(j, slot):
        return pltpu.make_async_remote_copy(
            src_ref=ow_all.at[slot], dst_ref=ow_all.at[slot], send_sem=ow_s.at[j - 1], recv_sem=ow_r.at[j - 1],
            device_id={"mp": lax.rem(x + j, mp)}, device_id_type=MESH,
        )

    for j in range(1, mp):
        ow_copy(j, x).start()

    loads[1].wait()
    for i in range(sub * half // 128):
        tcol[i * 128 : (i + 1) * 128, :] = to_col(tgt_ref[i : i + 1, :].astype(F32))
    bcol[...] = to_col(list_ref[pl.ds(z, 1), :].astype(F32))
    m_ref[...] = jnp.full(m_ref.shape, FLOOR, F32)
    l_ref[...] = jnp.zeros(l_ref.shape, F32)
    p_ref[...] = jnp.zeros(p_ref.shape, F32)
    acc[...] = jnp.zeros(acc.shape, F32)
    ends = []
    so_far = 0
    for u in range(utts):
        so_far = so_far + utt_ref[0, u]
        ends.append(so_far)

    def process(origin, h):
        across(origin, h, other).wait_recv()
        k = keys[origin, h].reshape(both, width)
        shard = (origin * mp + x) * (half_blocks * sub)
        place = lax.broadcasted_iota(jnp.int32, (1, both), 1)
        ids = shard + (place // ph) * half_blocks + h * (ph // BLK) + lax.rem(place, ph) // BLK
        listed = jnp.where(bcol[...] == ids.astype(F32), 1.0, 0.0)
        log_count = []
        for u in range(utts):
            count = jnp.sum(listed[u * per_utt : (u + 1) * per_utt, :], axis=0, keepdims=True)
            log_count.append(jnp.where(count > 0.5, jnp.log(jnp.maximum(count, 1.0)), HIDDEN_LOW))
        tok_first = shard * BLK // 128 + h * (ph // 128)
        tokens = jnp.concatenate(
            [
                tok_ref[pl.ds(tok_first + core * (own_half // 128) + i, 1), :]
                for core in range(sub)
                for i in range(ph // 128)
            ],
            axis=1,
        ).astype(F32)

        def rows_step(i, carry):
            rows = pl.ds(i * step_rows, step_rows)
            first = c * half + i * step_rows
            s = lax.dot_general(frames[rows, :], k, (((1,), (1,)), ((), ())), preferred_element_type=F32)
            frame_id = lax.broadcasted_iota(jnp.int32, (step_rows, both), 0) + first
            bias = jnp.broadcast_to(log_count[utts - 1], (step_rows, both))
            for u in range(utts - 2, -1, -1):
                bias = jnp.where(frame_id < ends[u], log_count[u], bias)
            s = s * scale + bias
            old = m_ref[rows, :]
            new = jnp.maximum(old, jnp.max(s, axis=1, keepdims=True))
            fade = jnp.exp(old - new)
            e = jnp.exp(s - new)
            hits = jnp.where(tokens == tcol[pl.ds(first, step_rows), :], e, 0.0)
            m_ref[rows, :] = new
            l_ref[rows, :] = l_ref[rows, :] * fade + lane_sum(e)
            p_ref[rows, :] = p_ref[rows, :] * fade + lane_sum(hits)
            acc[rows, :] = acc[rows, :] * fade + jnp.dot(e.astype(BF16), k, preferred_element_type=F32)
            return carry

        lax.fori_loop(0, half // step_rows, rows_step, 0)

    def own_step(h, carry):
        process(z, h)
        return carry

    lax.fori_loop(0, PIECES, own_step, 0)

    def gather_step(s, carry):
        t, h = s // PIECES, lax.rem(s, PIECES)
        from_left, from_right = z - 1 - t, z + 1 + t

        @pl.when(from_left >= 0)
        def _():
            right(s, from_left).wait_recv()

            @pl.when(z + 1 < packs)
            def _():
                right(s + PIECES, from_left).start()

            across(from_left, h, c).start()

        @pl.when(from_right < packs)
        def _():
            left(s, from_right).wait_recv()

            @pl.when(z > 0)
            def _():
                left(s + PIECES, from_right).start()

            across(from_right, h, c).start()

        @pl.when(from_left >= 0)
        def _():
            process(from_left, h)

        @pl.when(from_right < packs)
        def _():
            process(from_right, h)

        return carry

    lax.fori_loop(0, (packs - 1) * PIECES, gather_step, 0)

    def sums(rows):
        return (
            jnp.sum(l_ref[rows, :], axis=1, keepdims=True),
            jnp.sum(p_ref[rows, :], axis=1, keepdims=True),
        )

    def move(j, i):
        src = s2_send.at[j - 1] if i == per else c2_send.at[j - 1, pl.ds(i * lanes, lanes), :]
        dst = s2_recv.at[j - 1] if i == per else c2_recv.at[j - 1, pl.ds(i * lanes, lanes), :]
        spot = (j - 1) * (per + 1) + i
        return pltpu.make_async_remote_copy(
            src_ref=src, dst_ref=dst, send_sem=x2_s.at[spot], recv_sem=x2_r.at[spot],
            device_id={"mp": lax.rem(x + j, mp)}, device_id_type=MESH,
        )

    for j in range(1, mp):
        target = lax.rem(x + j, mp)
        for i in range(per):
            rows = pl.ds(target * part + i * lanes, lanes)
            c2_send[j - 1, i * lanes : (i + 1) * lanes, :] = acc[rows, :].astype(BF16)
            move(j, i).start()
            if i == 0:
                for b in range(per):
                    cut = pl.ds(target * part + b * lanes, lanes)
                    total, pointer = sums(cut)
                    s2_send[j - 1, 0, b : b + 1, :] = to_row(m_ref[cut, :])
                    s2_send[j - 1, 1, b : b + 1, :] = to_row(total)
                    s2_send[j - 1, 2, b : b + 1, :] = to_row(pointer)
                move(j, per).start()

    chunk = min(512, vcols)

    def vocabulary(g, i):
        h = hid[pl.ds(g * part + i * lanes, lanes), :]
        target = tcol[pl.ds(g * half + x * part + i * lanes, lanes), :]
        top = jnp.full((lanes, 128), FLOOR, F32)
        total = jnp.zeros((lanes, 128), F32)
        chosen = jnp.zeros((lanes, 128), F32)
        for q in range(mp):
            for v in range(vcols // chunk):
                w = ow_all[q, :, v * chunk : (v + 1) * chunk]
                logits = jnp.dot(h, w, preferred_element_type=F32)
                first_col = (q * sub + c) * vcols + v * chunk
                ids = (lax.broadcasted_iota(jnp.int32, (1, chunk), 1) + first_col).astype(F32)
                chosen = chosen + lane_sum(jnp.where(ids == target, logits, 0.0))
                new = top
                for b in range(chunk // 128):
                    new = jnp.maximum(new, logits[:, b * 128 : (b + 1) * 128])
                total = total * jnp.exp(top - new)
                for b in range(chunk // 128):
                    total = total + jnp.exp(logits[:, b * 128 : (b + 1) * 128] - new)
                top = new
        row_top = jnp.max(top, axis=1, keepdims=True)
        row_sum = jnp.sum(total * jnp.exp(top - row_top), axis=1, keepdims=True)
        row_hit = jnp.sum(chosen, axis=1, keepdims=True)
        st3[me, g * 3, i : i + 1, :] = to_row(row_top)
        st3[me, g * 3 + 1, i : i + 1, :] = to_row(row_sum)
        st3[me, g * 3 + 2, i : i + 1, :] = to_row(row_hit)

    def hid_copy(i, core):
        block = hid.at[pl.ds(core * part + i * lanes, lanes), :]
        return to_other(block, block, h_s.at[i], h_r.at[i])

    own_sums = [sums(pl.ds(x * part + i * lanes, lanes)) for i in range(per)]
    for j in range(1, mp):
        ow_copy(j, lax.rem(x + mp - j, mp)).wait_recv()
    for j in range(1, mp):
        move(j, per).wait_recv()
    for i in range(per):
        rows = pl.ds(x * part + i * lanes, lanes)
        total, pointer = own_sums[i]
        top = m_ref[rows, :]
        context = acc[rows, :]
        for j in range(1, mp):
            theirs, their_total, their_pointer = [to_col(s2_recv[j - 1, k, i : i + 1, :]) for k in range(3)]
            new = jnp.maximum(top, theirs)
            a, b = jnp.exp(top - new), jnp.exp(theirs - new)
            top = new
            total = total * a + their_total * b
            pointer = pointer * a + their_pointer * b
            move(j, i).wait_recv()
            context = context * a + c2_recv[j - 1, i * lanes : (i + 1) * lanes, :].astype(F32) * b
        hidden = jnp.tanh(frames[rows, :].astype(F32) + context / total).astype(BF16)
        hid[pl.ds(c * part + i * lanes, lanes), :] = hidden
        hid_copy(i, c).start()
        gate = jnp.sum(hidden.astype(F32) * gw_ref[...], axis=1, keepdims=True)
        st3[me, 3 * sub, i : i + 1, :] = to_row(gate)
        st3[me, 3 * sub + 1, i : i + 1, :] = to_row(pointer / total)
        vocabulary(c, i)
        hid_copy(i, other).wait_recv()
        vocabulary(other, i)

    def share(j, slot):
        return pltpu.make_async_remote_copy(
            src_ref=st3.at[slot], dst_ref=st3.at[slot], send_sem=t_s.at[j - 1], recv_sem=t_r.at[j - 1],
            device_id=peer(j), device_id_type=MESH,
        )

    for j in range(1, plane):
        share(j, me).start()
    for j in range(1, plane):
        share(j, lax.rem(me + plane - j, plane)).wait_recv()

    for q in range(mp):
        for g in range(sub):
            one, two = q * sub, q * sub + 1
            top_a, top_b = st3[one, g * 3], st3[two, g * 3]
            top = jnp.maximum(top_a, top_b)
            total = st3[one, g * 3 + 1] * jnp.exp(top_a - top) + st3[two, g * 3 + 1] * jnp.exp(top_b - top)
            log_norm = top + jnp.log(total)
            hit = st3[one, g * 3 + 2] + st3[two, g * 3 + 2]
            gate = 1.0 / (1.0 + jnp.exp(-st3[q * sub + g, 3 * sub]))
            mixed = (1.0 - gate) * jnp.exp(hit - log_norm) + gate * st3[q * sub + g, 3 * sub + 1]
            first_row = (g * mp + q) * per
            out_ref[first_row : first_row + per, :] = -jnp.log(mixed)

    def send_waits(s, carry):
        t = s // PIECES

        @pl.when((z >= t) & (z + 1 < packs))
        def _():
            right(s, z - t).wait_send()

        @pl.when((z + t < packs) & (z > 0))
        def _():
            left(s, z + t).wait_send()

        return carry

    lax.fori_loop(0, (packs - 1) * PIECES, send_waits, 0)

    def core_waits(s, carry):
        across(s // PIECES, lax.rem(s, PIECES), c).wait_send()
        return carry

    lax.fori_loop(0, packs * PIECES, core_waits, 0)
    for i in range(per):
        hid_copy(i, c).wait_send()
    for j in range(1, mp):
        ow_copy(j, x).wait_send()
        for i in range(per + 1):
            move(j, i).wait_send()
    for j in range(1, plane):
        share(j, me).wait_send()


def per_device(
    frame_enc, phrase_enc, key_weight, out_weight, gate_weight,
    phrase_token, bias_blocks, utt_lengths, targets,
):
    packs = lax.axis_size("pack")
    mp = lax.axis_size("mp")
    sub = lax.axis_size("sub")
    plane = mp * sub
    fr, width = frame_enc.shape
    depth = phrase_enc.shape[1]
    own_half = phrase_enc.shape[0] // sub
    vcols = out_weight.shape[1]
    half = fr // sub
    part = half // mp
    lanes = min(part, 128)
    entries = bias_blocks.shape[1]
    hops = (packs - 1) * PIECES
    others = max(mp - 1, 1)
    vmem = pltpu.VMEM
    dma = pltpu.SemaphoreType.DMA
    any_spec = pl.BlockSpec(memory_space=pl.ANY)
    vmem_spec = pl.BlockSpec(memory_space=vmem)
    smem_spec = pl.BlockSpec(memory_space=pltpu.SMEM)
    out = pl.pallas_call(
        functools.partial(kernel, (packs, mp, sub, lanes)),
        out_shape=jax.ShapeDtypeStruct((fr // lanes, lanes), F32),
        in_specs=[any_spec] * 4 + [vmem_spec] * 3 + [smem_spec, vmem_spec],
        out_specs=vmem_spec,
        scratch_shapes=[
            vmem((half, width), BF16),
            vmem((own_half, depth), BF16),
            vmem((depth, width), BF16),
            vmem((packs, PIECES, sub, own_half // PIECES, width), BF16),
            vmem((mp, width, vcols), BF16),
            vmem((fr, 1), F32),
            vmem((entries, 1), F32),
            vmem((half, 1), F32),
            vmem((half, 128), F32),
            vmem((half, 128), F32),
            vmem((half, width), F32),
            vmem((others, part, width), BF16),
            vmem((others, part, width), BF16),
            vmem((others, 3, part // lanes, lanes), F32),
            vmem((others, 3, part // lanes, lanes), F32),
            vmem((sub * part, width), BF16),
            vmem((plane, 3 * sub + 2, part // lanes, lanes), F32),
            dma((3 + PIECES,)), dma((hops,)), dma((hops,)), dma((hops,)), dma((hops,)),
            dma((packs * PIECES,)), dma((packs * PIECES,)),
            dma((others,)), dma((others,)),
            dma((others * (part // lanes + 1),)), dma((others * (part // lanes + 1),)),
            dma((part // lanes,)), dma((part // lanes,)),
            dma((plane - 1,)), dma((plane - 1,)),
        ],
        compiler_params=pltpu.CompilerParams(
            collective_id=0, has_side_effects=True, vmem_limit_bytes=56 * 1024 * 1024
        ),
    )(
        frame_enc, phrase_enc, key_weight, out_weight,
        gate_weight.reshape(1, width),
        phrase_token.reshape(-1, 128),
        bias_blocks, utt_lengths,
        targets.reshape(-1, 128),
    )
    return out.reshape(fr)


def solution(mesh):
    in_specs = (
        P(("groups", "pack"), None),
        P(("groups", "pack", "mp"), None),
        P(),
        P(None, ("mp", "sub")),
        P(),
        P("groups"),
        P("groups", None),
        P(("groups", "pack"), None),
        P(("groups", "pack")),
    )
    return jax.shard_map(
        per_device, mesh=mesh, in_specs=in_specs, out_specs=P(("groups", "pack")), check_vma=False
    )
```

time: 61.5 us -> 61.6 us (level)
  no operation moved by 1% of the time
where the time goes in v2:
time: 61.6 us; the launch traced here: 61.4 us
  Pallas kernels  60.1 us (98%)
  local copies, waits for them, and re-layouts  1.28 us (2%)
    pallas_call x1, Pallas kernels, per_device(): pl.pallas_call(functools.partial(kernel, (packs, mp, sub, lanes)), out_sh...  60.1 us
    unnamed x1, local copies, waits for them, and re-layouts  1.28 us

profile of v2, /device:TPU:0, one launch (start us, length us, event | category | flops | bytes accessed | tf_op | source)
XLA Modules:
  0.0 61.4 jit_solution(13955309033995267040)
XLA Ops:
  0.0 60.1 %shard_map.91 = f32[8,128]{1,0:T(8,128)} custom-call(bf16[1024,512]{1,0:T(8,128)(2,1)} %frame_hbm.1, bf16[1024,1024]{1,0:T(8,128)(2,1)} %phrase_hbm.1, bf16[1024,512]{1,0:T(8,128)(2,1)} %kw_hbm.1, bf16[512,1024]{1,0:T(8,128)(2,1)} %ow_hbm.1, f32[1,512]{1,0:T(1,128)} %bitcast.7, s32[64,128]{1,0:T(8,128)} %bitcast.4, s32[4,128]{1,0:T(4,128)} %list_ref.1, ...), custom_call_target="tpu_custom_call" | custom-call | tf_op jit(solution)/shard_map/pallas_call | solution.py:427
  60.1 1.3 %copy.11 = f32[1024]{0:T(1024)} copy(f32[1024]{0:T(1024)} %bitcast.5) | data formatting | bytes 8192

commit v3 on v2

--- a/solution.py
+++ b/solution.py
@@ -42,7 +42,7 @@
     dims,
     frame_hbm, phrase_hbm, kw_hbm, ow_hbm, gw_ref, tok_ref, list_ref, utt_ref, tgt_ref,
     out_ref,
-    frames, phrase, kw, keys, ow_all, tcol, bcol, m_ref, l_ref, p_ref, acc,
+    frames, phrase, kw, keys, ow_all, tcol, bcol, log_count, tokens, m_ref, l_ref, p_ref, acc,
     c2_send, c2_recv, s2_send, s2_recv, hid, st3,
     load_sem, rs, rr, ls, lr, cs, cr, ow_s, ow_r, x2_s, x2_r, h_s, h_r, t_s, t_r,
 ):
@@ -170,19 +170,22 @@
         so_far = so_far + utt_ref[0, u]
         ends.append(so_far)
 
-    def process(origin, h):
-        across(origin, h, other).wait_recv()
-        k = keys[origin, h].reshape(both, width)
+    owner = (
+        lax.broadcasted_iota(jnp.int32, (8, entries), 1) // per_utt
+        == lax.broadcasted_iota(jnp.int32, (8, entries), 0)
+    )
+    owner = jnp.where(owner, 1.0, 0.0).astype(BF16)
+
+    def table_step(spot, carry):
+        origin, h = spot // PIECES, lax.rem(spot, PIECES)
         shard = (origin * mp + x) * (half_blocks * sub)
         place = lax.broadcasted_iota(jnp.int32, (1, both), 1)
         ids = shard + (place // ph) * half_blocks + h * (ph // BLK) + lax.rem(place, ph) // BLK
-        listed = jnp.where(bcol[...] == ids.astype(F32), 1.0, 0.0)
-        log_count = []
-        for u in range(utts):
-            count = jnp.sum(listed[u * per_utt : (u + 1) * per_utt, :], axis=0, keepdims=True)
-            log_count.append(jnp.where(count > 0.5, jnp.log(jnp.maximum(count, 1.0)), HIDDEN_LOW))
+        listed = jnp.where(bcol[...] == ids.astype(F32), 1.0, 0.0).astype(BF16)
+        count = jnp.dot(owner, listed, preferred_element_type=F32)
+        log_count[spot] = jnp.where(count > 0.5, jnp.log(jnp.maximum(count, 1.0)), HIDDEN_LOW)
         tok_first = shard * BLK // 128 + h * (ph // 128)
-        tokens = jnp.concatenate(
+        tokens[spot] = jnp.concatenate(
             [
                 tok_ref[pl.ds(tok_first + core * (own_half // 128) + i, 1), :]
                 for core in range(sub)
@@ -190,21 +193,29 @@
             ],
             axis=1,
         ).astype(F32)
+        return carry
+
+    lax.fori_loop(0, packs * PIECES, table_step, 0)
+
+    def process(origin, h):
+        across(origin, h, other).wait_recv()
+        k = keys[origin, h].reshape(both, width)
+        spot = origin * PIECES + h
 
         def rows_step(i, carry):
             rows = pl.ds(i * step_rows, step_rows)
             first = c * half + i * step_rows
             s = lax.dot_general(frames[rows, :], k, (((1,), (1,)), ((), ())), preferred_element_type=F32)
             frame_id = lax.broadcasted_iota(jnp.int32, (step_rows, both), 0) + first
-            bias = jnp.broadcast_to(log_count[utts - 1], (step_rows, both))
+            bias = jnp.broadcast_to(log_count[spot, utts - 1 : utts, :], (step_rows, both))
             for u in range(utts - 2, -1, -1):
-                bias = jnp.where(frame_id < ends[u], log_count[u], bias)
+                bias = jnp.where(frame_id < ends[u], log_count[spot, u : u + 1, :], bias)
             s = s * scale + bias
             old = m_ref[rows, :]
             new = jnp.maximum(old, jnp.max(s, axis=1, keepdims=True))
             fade = jnp.exp(old - new)
             e = jnp.exp(s - new)
-            hits = jnp.where(tokens == tcol[pl.ds(first, step_rows), :], e, 0.0)
+            hits = jnp.where(tokens[spot] == tcol[pl.ds(first, step_rows), :], e, 0.0)
             m_ref[rows, :] = new
             l_ref[rows, :] = l_ref[rows, :] * fade + lane_sum(e)
             p_ref[rows, :] = p_ref[rows, :] * fade + lane_sum(hits)
@@ -213,17 +224,13 @@
 
         lax.fori_loop(0, half // step_rows, rows_step, 0)
 
-    def own_step(h, carry):
-        process(z, h)
-        return carry
-
-    lax.fori_loop(0, PIECES, own_step, 0)
+    hops = (packs - 1) * PIECES
 
     def gather_step(s, carry):
-        t, h = s // PIECES, lax.rem(s, PIECES)
+        t = s // PIECES
         from_left, from_right = z - 1 - t, z + 1 + t
 
-        @pl.when(from_left >= 0)
+        @pl.when((s < hops) & (from_left >= 0))
         def _():
             right(s, from_left).wait_recv()
 
@@ -231,9 +238,9 @@
             def _():
                 right(s + PIECES, from_left).start()
 
-            across(from_left, h, c).start()
-
-        @pl.when(from_right < packs)
+            across(from_left, lax.rem(s, PIECES), c).start()
+
+        @pl.when((s < hops) & (from_right < packs))
         def _():
             left(s, from_right).wait_recv()
 
@@ -241,19 +248,26 @@
             def _():
                 left(s + PIECES, from_right).start()
 
-            across(from_right, h, c).start()
-
-        @pl.when(from_left >= 0)
-        def _():
-            process(from_left, h)
-
-        @pl.when(from_right < packs)
-        def _():
-            process(from_right, h)
+            across(from_right, lax.rem(s, PIECES), c).start()
+
+        @pl.when(s < PIECES)
+        def _():
+            process(z, s)
+
+        before = s - 1
+        ago, h = before // PIECES, lax.rem(before, PIECES)
+
+        @pl.when((s > 0) & (z - 1 - ago >= 0))
+        def _():
+            process(z - 1 - ago, h)
+
+        @pl.when((s > 0) & (z + 1 + ago < packs))
+        def _():
+            process(z + 1 + ago, h)
 
         return carry
 
-    lax.fori_loop(0, (packs - 1) * PIECES, gather_step, 0)
+    lax.fori_loop(0, hops + 1, gather_step, 0)
 
     def sums(rows):
         return (
@@ -437,6 +451,8 @@
             vmem((mp, width, vcols), BF16),
             vmem((fr, 1), F32),
             vmem((entries, 1), F32),
+            vmem((packs * PIECES, 8, sub * own_half // PIECES), F32),
+            vmem((packs * PIECES, 1, sub * own_half // PIECES), F32),
             vmem((half, 1), F32),
             vmem((half, 128), F32),
             vmem((half, 128), F32),

time: 61.6 us -> 59.1 us (0.959)
  Pallas kernels: 60.1 us -> 57.6 us
    pallas_call x1, Pallas kernels: 60.1 us -> 57.6 us  [per_device(): pl.pallas_call(functools.partial(kernel, (packs, mp, sub, lanes)), out_sh...]
where the time goes in v3:
time: 59.1 us; the launch traced here: 58.9 us
  Pallas kernels  57.6 us (97%)
  local copies, waits for them, and re-layouts  1.28 us (2%)
    pallas_call x1, Pallas kernels, per_device(): pl.pallas_call(functools.partial(kernel, (packs, mp, sub, lanes)), out_sh...  57.6 us
    unnamed x1, local copies, waits for them, and re-layouts  1.28 us

profile of v3, /device:TPU:0, one launch (start us, length us, event | category | flops | bytes accessed | tf_op | source)
XLA Modules:
  0.0 58.9 jit_solution(17602613957844114514)
XLA Ops:
  0.0 57.6 %shard_map.91 = f32[8,128]{1,0:T(8,128)} custom-call(bf16[1024,512]{1,0:T(8,128)(2,1)} %frame_hbm.1, bf16[1024,1024]{1,0:T(8,128)(2,1)} %phrase_hbm.1, bf16[1024,512]{1,0:T(8,128)(2,1)} %kw_hbm.1, bf16[512,1024]{1,0:T(8,128)(2,1)} %ow_hbm.1, f32[1,512]{1,0:T(1,128)} %bitcast.7, s32[64,128]{1,0:T(8,128)} %bitcast.4, s32[4,128]{1,0:T(4,128)} %list_ref.1, ...), custom_call_target="tpu_custom_call" | custom-call | tf_op jit(solution)/shard_map/pallas_call | solution.py:441
  57.6 1.3 %copy.11 = f32[1024]{0:T(1024)} copy(f32[1024]{0:T(1024)} %bitcast.5) | data formatting | bytes 8192

commit v4 on v3

--- a/solution.py
+++ b/solution.py
@@ -16,7 +16,7 @@
 F32 = jnp.float32
 BF16 = jnp.bfloat16
 PIECES = 4
-ROWS = 256
+ROWS = 512
 
 
 def eye(n):
@@ -63,7 +63,7 @@
     half_blocks = own_half // BLK
     scale = GAIN / math.sqrt(width)
     per = part // lanes
-    step_rows = min(ROWS, part)
+    step_rows = min(ROWS, half)
 
     barrier = pltpu.get_barrier_semaphore()
 

time: 59.1 us -> 58.6 us (level)
  no operation moved by 1% of the time
where the time goes in v4:
time: 58.6 us; the launch traced here: 58.4 us
  Pallas kernels  57.1 us (97%)
  local copies, waits for them, and re-layouts  1.28 us (2%)
    pallas_call x1, Pallas kernels, per_device(): pl.pallas_call(functools.partial(kernel, (packs, mp, sub, lanes)), out_sh...  57.1 us
    unnamed x1, local copies, waits for them, and re-layouts  1.28 us

profile of v4, /device:TPU:0, one launch (start us, length us, event | category | flops | bytes accessed | tf_op | source)
XLA Modules:
  0.0 58.4 jit_solution(9582460124958647964)
XLA Ops:
  0.0 57.1 %shard_map.91 = f32[8,128]{1,0:T(8,128)} custom-call(bf16[1024,512]{1,0:T(8,128)(2,1)} %frame_hbm.1, bf16[1024,1024]{1,0:T(8,128)(2,1)} %phrase_hbm.1, bf16[1024,512]{1,0:T(8,128)(2,1)} %kw_hbm.1, bf16[512,1024]{1,0:T(8,128)(2,1)} %ow_hbm.1, f32[1,512]{1,0:T(1,128)} %bitcast.7, s32[64,128]{1,0:T(8,128)} %bitcast.4, s32[4,128]{1,0:T(4,128)} %list_ref.1, ...), custom_call_target="tpu_custom_call" | custom-call | tf_op jit(solution)/shard_map/pallas_call | solution.py:441
  57.1 1.3 %copy.11 = f32[1024]{0:T(1024)} copy(f32[1024]{0:T(1024)} %bitcast.5) | data formatting | bytes 8192
